TPU v7x, 32 devices: a whole 2x2x4 slice. The times are simulated.
32 devices in a mesh: groups: 2 (over y), seq: 8 (over z, x), head: 1, sub: 2 (over core).
Axes of the slice: x: 2, y: 2, z: 4, core: 2. Of those that a mesh axis runs over, the one named last changes fastest.
Arguments:
- queries: bfloat16 [8, 32768, 512], P('head', ('groups', 'seq', 'sub')), parts along dimension 1, may hold values from -6 to 6
- keys: bfloat16 [8, 32768, 512], P('head', ('groups', 'seq', 'sub')), parts along dimension 1, may hold values from -6 to 6
- values: bfloat16 [8, 32768, 512], P('head', ('groups', 'seq', 'sub')), parts along dimension 1, may hold values from -6 to 6
- lr_codes: int32 [8, 32768], P('head', ('groups', 'seq', 'sub')), parts along dimension 1, may hold values from 0 to 15
- fast_gate: float32 [8, 512, 512], P('head', ('seq', 'sub')), may hold values from -0.25 to 0.25
- fast_up: float32 [8, 512, 512], P('head', ('seq', 'sub')), may hold values from -0.25 to 0.25
- fast_down: float32 [8, 512, 512], P('head', ('seq', 'sub')), may hold values from -0.25 to 0.25
Outputs:
- fast_out: bfloat16 [8, 32768, 512], P('head', ('groups', 'seq', 'sub')), parts along dimension 1
There are 2 independent parts, one for each index of `groups`. A program takes and returns all parts, laid end to end along the dimension named above; an argument that names none is the same for every part. Nothing has to cross between parts.
All inputs are finite; a program needn't handle non-finite values.
Results may differ from a plain program's by a relative error of at most 0.0085.
Values may be sent and summed in bfloat16 or wider, within the bound.
A program may use at most 192 MiB of HBM per device.

v0:
```python
import jax
import jax.numpy as jnp
from jax import lax
from jax.sharding import PartitionSpec as P

EPSILON = 1e-06
STEP_SIZE = 0.5


def column_squares(matrix):
    return jnp.sum(matrix * matrix, axis=1)


def rescale(moved, col_weight, col_moved):
    return moved * jnp.sqrt((col_weight + EPSILON) / (col_moved + EPSILON))[:, None, :]


def step_scale(col_weight, grad_total):
    return (
        STEP_SIZE * jnp.sqrt(jnp.sum(col_weight, axis=1) + EPSILON) / jnp.sqrt(grad_total + EPSILON)
    )


def apply_fast(queries, gate_b, up_b, down_b):
    query_gate = jnp.einsum("htd,hdf->htf", queries, gate_b, preferred_element_type=jnp.float32)
    query_up = jnp.einsum("htd,hdf->htf", queries, up_b, preferred_element_type=jnp.float32)
    query_hidden = (jax.nn.silu(query_gate) * query_up).astype(jnp.bfloat16)
    return jnp.einsum(
        "htf,hfd->htd", query_hidden, down_b, preferred_element_type=jnp.float32
    ).astype(jnp.bfloat16)


def local_grads(keys, target, gate_b, up_b, down_b):
    gate_pre = jnp.einsum("htd,hdf->htf", keys, gate_b, preferred_element_type=jnp.float32)
    up_pre = jnp.einsum("htd,hdf->htf", keys, up_b, preferred_element_type=jnp.float32)
    sigmoid_gate = jax.nn.sigmoid(gate_pre)
    hidden = (gate_pre * sigmoid_gate * up_pre).astype(jnp.bfloat16)
    back = jnp.einsum("htd,hfd->htf", target, down_b, preferred_element_type=jnp.float32)
    grad_gate_pre = (back * up_pre * sigmoid_gate * (1.0 + gate_pre * (1.0 - sigmoid_gate))).astype(
        jnp.bfloat16
    )
    grad_up_pre = (back * gate_pre * sigmoid_gate).astype(jnp.bfloat16)
    grad_gate = jnp.einsum("htd,htf->hdf", keys, grad_gate_pre, preferred_element_type=jnp.float32)
    grad_up = jnp.einsum("htd,htf->hdf", keys, grad_up_pre, preferred_element_type=jnp.float32)
    grad_down = jnp.einsum("htf,htd->hfd", hidden, target, preferred_element_type=jnp.float32)
    return (grad_gate, grad_up, grad_down)


def on_device(queries, keys, values, lr_codes, fast_gate, fast_up, fast_down):
    token_rates = (lr_codes.astype(jnp.float32) + 1.0) / 16.0
    target = (-token_rates[:, :, None] * values.astype(jnp.float32)).astype(jnp.bfloat16)
    gate_b, up_b, down_b = (
        lax.all_gather(fast_gate.astype(jnp.bfloat16), ("seq", "sub"), axis=1, tiled=True),
        lax.all_gather(fast_up.astype(jnp.bfloat16), ("seq", "sub"), axis=1, tiled=True),
        lax.all_gather(fast_down.astype(jnp.bfloat16), ("seq", "sub"), axis=1, tiled=True),
    )
    grad_gate, grad_up, grad_down = local_grads(keys, target, gate_b, up_b, down_b)
    owned = (
        lax.psum_scatter(grad_gate, ("seq", "sub"), scatter_dimension=1, tiled=True),
        lax.psum_scatter(grad_up, ("seq", "sub"), scatter_dimension=1, tiled=True),
        lax.psum_scatter(grad_down, ("seq", "sub"), scatter_dimension=1, tiled=True),
    )
    weights = (fast_gate, fast_up, fast_down)
    grad_local = jnp.stack(
        [
            jnp.sum(owned[0] * owned[0], axis=(1, 2)),
            jnp.sum(owned[1] * owned[1], axis=(1, 2)),
            jnp.sum(owned[2] * owned[2], axis=(1, 2)),
        ],
        axis=1,
    )
    col_gate, col_up, col_down, grad_totals = lax.psum(
        (column_squares(fast_gate), column_squares(fast_up), column_squares(fast_down), grad_local),
        ("seq", "sub"),
    )
    col_weights = (col_gate, col_up, col_down)
    moved_all = []
    for index in range(3):
        scale = step_scale(col_weights[index], grad_totals[:, index])
        moved_all.append(weights[index] - scale[:, None, None] * owned[index])
    moved_cols = lax.psum(
        (column_squares(moved_all[0]), column_squares(moved_all[1]), column_squares(moved_all[2])),
        ("seq", "sub"),
    )
    renewed = [
        rescale(moved_all[index], col_weights[index], moved_cols[index]).astype(jnp.bfloat16)
        for index in range(3)
    ]
    new_gate, new_up, new_down = (
        lax.all_gather(renewed[0], ("seq", "sub"), axis=1, tiled=True),
        lax.all_gather(renewed[1], ("seq", "sub"), axis=1, tiled=True),
        lax.all_gather(renewed[2], ("seq", "sub"), axis=1, tiled=True),
    )
    return apply_fast(queries, new_gate, new_up, new_down)


def solution(mesh):
    return jax.shard_map(
        on_device,
        mesh=mesh,
        in_specs=(
            P("head", ("groups", "seq", "sub"), None),
            P("head", ("groups", "seq", "sub"), None),
            P("head", ("groups", "seq", "sub"), None),
            P("head", ("groups", "seq", "sub")),
            P("head", ("seq", "sub"), None),
            P("head", ("seq", "sub"), None),
            P("head", ("seq", "sub"), None),
        ),
        out_specs=P("head", ("groups", "seq", "sub"), None),
        check_vma=False,
    )
```

profile of v0, /device:TPU:0, one launch (start us, length us, event | category | flops | bytes accessed | tf_op | source)
XLA Modules:
  0.0 794.0 jit_solution(1773407533182401554)
XLA Ops:
  6.5 2.6 multiply_reduce_fusion.8
  9.2 2.6 multiply_reduce_fusion.1
  11.8 2.6 multiply_reduce_fusion.3
  15.3 47.5 %all-gather.11.cloned.1.call-done = bf16[8,512,512]{2,1,0:T(8,128)(2,1)} async-done(((bf16[8,32,512]{2,1,0:T(8,128)(2,1)}), bf16[8,512,512]{2,1,0:T(8,128)(2,1)}) %all-gather.11.cloned.1.call-update) | async-done | bytes 4194320 | tf_op jit(solution)/shard_map/all_gather | solution.py:53
  62.9 14.8 %fusion.19 = f32[8,1024,512]{2,1,0:T(8,128)} fusion(bf16[8,1024,512]{2,1,0:T(8,128)(2,1)} %param.8, bf16[8,512,512]{2,1,0:T(8,128)(2,1)} %all-gather.11.cloned.1.call-done), kind=kOutput, calls=%fused_computation.50 | convolution fusion | flops 4294967296 | bytes 29360128 | tf_op jit(solution)/shard_map/htd,hdf->htf/dot_general | solution.py:34
  77.7 36.5 %all-gather.7.cloned.1.call-done = bf16[8,512,512]{2,1,0:T(8,128)(2,1)} async-done(((bf16[8,32,512]{2,1,0:T(8,128)(2,1)}), bf16[8,512,512]{2,1,0:T(8,128)(2,1)}) %all-gather.7.cloned.1.call-update) | async-done | bytes 4194320 | tf_op jit(solution)/shard_map/all_gather | solution.py:55
  114.1 11.7 %fusion.7 = f32[8,1024,512]{2,1,0:T(8,128)} fusion(bf16[8,512,512]{2,1,0:T(8,128)(2,1)} %all-gather.7.cloned.1.call-done, bf16[8,1024,512]{2,1,0:T(8,128)(2,1)} %param.9, f32[8,1024]{1,0:T(8,128)S(1)} %multiply_negate_fusion), kind=kOutput, calls=%fused_computation.15 | convolution fusion | flops 4307550208 | bytes 29392896 | tf_op jit(solution)/shard_map/htd,hfd->htf/dot_general | solution.py:38
  125.8 19.5 %fusion.13 = f32[8,512,512]{1,2,0:T(8,128)} fusion(bf16[8,1024,512]{2,1,0:T(8,128)(2,1)} %param.8, f32[8,1024,512]{2,1,0:T(8,128)} %fusion.7, f32[8,1024,512]{2,1,0:T(8,128)} %fusion.19), kind=kOutput, calls=%fused_computation.21 | convolution fusion | flops 4320133120 | bytes 50331648 | tf_op jit(solution)/shard_map/htd,htf->hdf/dot_general | solution.py:44
  145.3 10.5 %copy.18 = f32[8,512,512]{2,0,1:T(8,128)} copy(f32[8,512,512]{1,2,0:T(8,128)} %fusion.13) | data formatting | bytes 16777216 | tf_op jit(solution)/shard_map/htd,htf->hdf/dot_general | solution.py:44
  156.0 9.4 %all-gather.9.cloned.1.call-done = bf16[8,512,512]{2,1,0:T(8,128)(2,1)} async-done(((bf16[8,32,512]{2,1,0:T(8,128)(2,1)}), bf16[8,512,512]{2,1,0:T(8,128)(2,1)}) %all-gather.9.cloned.1.call-update) | async-done | bytes 4194320 | tf_op jit(solution)/shard_map/all_gather | solution.py:54
  165.4 16.6 %fusion.18 = f32[8,1024,512]{2,1,0:T(8,128)} fusion(bf16[8,1024,512]{2,1,0:T(8,128)(2,1)} %param.8, bf16[8,512,512]{2,1,0:T(8,128)(2,1)} %all-gather.9.cloned.1.call-done), kind=kOutput, calls=%fused_computation.49 | convolution fusion | flops 4294967296 | bytes 29360128 | tf_op jit(solution)/shard_map/htd,hdf->htf/dot_general | solution.py:35
  182.0 21.8 %fusion.5 = f32[8,512,512]{2,1,0:T(8,128)} fusion(f32[8,1024,512]{2,1,0:T(8,128)} %fusion.18, f32[8,1024,512]{2,1,0:T(8,128)} %fusion.19, bf16[8,1024,512]{2,1,0:T(8,128)(2,1)} %param.9, f32[8,1024]{1,0:T(8,128)S(1)} %multiply_negate_fusion), kind=kOutput, calls=%fused_computation.13 | convolution fusion | flops 4332716032 | bytes 50364416 | tf_op jit(solution)/shard_map/htf,htd->hfd/dot_general | solution.py:45
  203.9 25.5 %fusion.12 = f32[8,512,512]{1,2,0:T(8,128)} fusion(bf16[8,1024,512]{2,1,0:T(8,128)(2,1)} %param.8, f32[8,1024,512]{2,1,0:T(8,128)} %fusion.19, f32[8,1024,512]{2,1,0:T(8,128)} %fusion.7, f32[8,1024,512]{2,1,0:T(8,128)} %fusion.18), kind=kOutput, calls=%fused_computation.20 | convolution fusion | flops 4336910336 | bytes 67108864 | tf_op jit(solution)/shard_map/htd,htf->hdf/dot_general | solution.py:43
  229.4 10.6 %copy.16 = f32[8,512,512]{2,0,1:T(8,128)} copy(f32[8,512,512]{1,2,0:T(8,128)} %fusion.12) | data formatting | bytes 16777216 | tf_op jit(solution)/shard_map/htd,htf->hdf/dot_general | solution.py:43
  240.1 32.5 %reduce-scatter.6.cloned.1.call-done = f32[8,32,512]{2,0,1:T(8,128)} async-done(((f32[8,512,512]{2,0,1:T(8,128)}), f32[8,32,512]{2,0,1:T(8,128)}) %reduce-scatter.6.cloned.1.call-update) | async-done | bytes 524304 | tf_op jit(solution)/shard_map/reduce_scatter | solution.py:60
  272.6 1.4 multiply_reduce_fusion.6
  273.9 107.0 %reduce-scatter.8.cloned.1.call-done = f32[8,32,512]{2,1,0:T(8,128)} async-done(((f32[8,512,512]{2,1,0:T(8,128)}), f32[8,32,512]{2,1,0:T(8,128)}) %reduce-scatter.8.cloned.1.call-update) | async-done | bytes 524304 | tf_op jit(solution)/shard_map/reduce_scatter | solution.py:61
  381.0 1.2 multiply_reduce_fusion.5
  382.2 107.2 %reduce-scatter.4.cloned.1.call-done = f32[8,32,512]{2,0,1:T(8,128)} async-done(((f32[8,512,512]{2,0,1:T(8,128)}), f32[8,32,512]{2,0,1:T(8,128)}) %reduce-scatter.4.cloned.1.call-update) | async-done | bytes 524304 | tf_op jit(solution)/shard_map/reduce_scatter | solution.py:59
  489.3 1.3 multiply_reduce_fusion.7
  490.7 60.4 %all-reduce.1 = (f32[8,3]{0,1:T(4,128)S(1)}, f32[8,512]{1,0:T(8,128)S(1)}, f32[8,512]{1,0:T(8,128)S(1)}, f32[8,512]{1,0:T(8,128)S(1)}) all-reduce(f32[8,3]{0,1:T(4,128)S(1)} %pad_maximum_fusion, f32[8,512]{1,0:T(8,128)S(1)} %copy-done.5, ...), channel_id=1, replica_groups=mesh['groups'=2,'seq'=8,'head'=1,'sub'=2] {'seq','sub'}, use_global_device_ids=true, to_apply=%region_9.0 | all-reduce | flops 12312 | bytes 98496 | tf_op jit(solution)/shard_map/psum | solution.py:72
  551.4 1.2 multiply_reduce_fusion
  552.7 1.9 multiply_reduce_fusion.2
  554.6 57.7 %all-reduce = (f32[8,512]{1,0:T(8,128)S(1)}, f32[8,512]{1,0:T(8,128)S(1)}, f32[8,512]{1,0:T(8,128)S(1)}) all-reduce(f32[8,512]{1,0:T(8,128)S(1)} %multiply_reduce_fusion, f32[8,512]{1,0:T(8,128)S(1)} %get-tuple-element.22, f32[8,512]{1,0:T(8,128)S(1)} %get-tuple-element.21), channel_id=1, replica_groups=mesh['groups'=2,'seq'=8,'head'=1,'sub'=2] {'seq','sub'}, use_global_device_ids=true, to_apply=%region_21.0 | all-reduce | flops 12288 | bytes 98304 | tf_op jit(solution)/shard_map/psum | solution.py:81
  612.3 2.1 multiply_convert_fusion.15
  614.5 1.9 multiply_convert_fusion.13
  616.7 1.0 multiply_convert_fusion.14
  617.7 44.6 %all-gather.13.cloned.1.call-done = bf16[8,512,512]{2,0,1:T(8,128)(2,1)} async-done(((bf16[8,32,512]{2,0,1:T(8,128)(2,1)}), bf16[8,512,512]{2,0,1:T(8,128)(2,1)}) %all-gather.13.cloned.1.call-update) | async-done | bytes 4194320 | tf_op jit(solution)/shard_map/all_gather | solution.py:90
  662.3 14.9 %fusion.10 = f32[8,512,1024]{1,2,0:T(8,128)} fusion(bf16[8,1024,512]{2,1,0:T(8,128)(2,1)} %param.7, bf16[8,512,512]{2,0,1:T(8,128)(2,1)} %all-gather.13.cloned.1.call-done), kind=kOutput, calls=%fused_computation.18 | convolution fusion | flops 4294967296 | bytes 29360128 | tf_op jit(solution)/shard_map/htd,hdf->htf/dot_general | solution.py:25
  677.3 36.4 %all-gather.17.cloned.1.call-done = bf16[8,512,512]{2,1,0:T(8,128)(2,1)} async-done(((bf16[8,32,512]{2,1,0:T(8,128)(2,1)}), bf16[8,512,512]{2,1,0:T(8,128)(2,1)}) %all-gather.17.cloned.1.call-update) | async-done | bytes 4194320 | tf_op jit(solution)/shard_map/all_gather | solution.py:92
  713.6 51.2 %all-gather.15.cloned.1.call-done = bf16[8,512,512]{2,0,1:T(8,128)(2,1)} async-done(((bf16[8,32,512]{2,0,1:T(8,128)(2,1)}), bf16[8,512,512]{2,0,1:T(8,128)(2,1)}) %all-gather.15.cloned.1.call-update) | async-done | bytes 4194320 | tf_op jit(solution)/shard_map/all_gather | solution.py:91
  764.9 22.5 %convolution_convert_fusion = bf16[8,1024,512]{2,1,0:T(8,128)(2,1)} fusion(bf16[8,512,512]{2,1,0:T(8,128)(2,1)} %all-gather.17.cloned.1.call-done, f32[8,512,1024]{1,2,0:T(8,128)} %fusion.10, bf16[8,1024,512]{2,1,0:T(8,128)(2,1)} %param.7, bf16[8,512,512]{2,0,1:T(8,128)(2,1)} %all-gather.15.cloned.1.call-done), kind=kOutput, calls=%fused_computation.16 | convolution fusion | flops 8619294720 | bytes 41943040 | tf_op jit(solution)/shard_map/htf,hfd->htd/dot_general | solution.py:28
  (41 shorter events, 2.1 us)
Async XLA Ops:
  6.5 56.3 %all-gather.11.cloned.1.call-start = ((), (), s32[]{:S(2)}) async-start(), calls=%async_computation.5 | async-start | bytes 4456448 | tf_op jit(solution)/shard_map/all_gather | solution.py:53
  9.1 105.0 %all-gather.7.cloned.1.call-start = ((), (), s32[]{:S(2)}) async-start(), calls=%async_computation.3 | async-start | bytes 4456448 | tf_op jit(solution)/shard_map/all_gather | solution.py:55
  11.8 153.7 %all-gather.9.cloned.1.call-start = ((), (), s32[]{:S(2)}) async-start(), calls=%async_computation.4 | async-start | bytes 4456448 | tf_op jit(solution)/shard_map/all_gather | solution.py:54
  14.5 258.1 %reduce-scatter.6.cloned.1.call-start = ((), (), s32[]{:S(2)}) async-start(), calls=%async_computation.7 | async-start | bytes 8912896 | tf_op jit(solution)/shard_map/reduce_scatter | solution.py:60
  155.8 225.2 %reduce-scatter.8.cloned.1.call-start = ((), (), s32[]{:S(2)}) async-start(), calls=%async_computation.8 | async-start | bytes 8912896 | tf_op jit(solution)/shard_map/reduce_scatter | solution.py:61
  203.8 285.5 %reduce-scatter.4.cloned.1.call-start = ((), (), s32[]{:S(2)}) async-start(), calls=%async_computation.6 | async-start | bytes 8912896 | tf_op jit(solution)/shard_map/reduce_scatter | solution.py:59
  240.0 250.7 %copy-start.4 = (f32[8,512]{1,0:T(8,128)S(1)}, f32[8,512]{1,0:T(8,128)}, u32[]{:S(2)}) copy-start(f32[8,512]{1,0:T(8,128)} %get-tuple-element.14) | copy-start | bytes 49156
  240.0 250.7 %copy-start.5 = (f32[8,512]{1,0:T(8,128)S(1)}, f32[8,512]{1,0:T(8,128)}, u32[]{:S(2)}) copy-start(f32[8,512]{1,0:T(8,128)} %get-tuple-element.16) | copy-start | bytes 49156
  240.0 250.7 %copy-start.6 = (f32[8,512]{1,0:T(8,128)S(1)}, f32[8,512]{1,0:T(8,128)}, u32[]{:S(2)}) copy-start(f32[8,512]{1,0:T(8,128)} %get-tuple-element.12) | copy-start | bytes 49156
  240.0 311.4 %copy-start = (f32[8,32,512]{2,1,0:T(8,128)S(1)}, f32[8,32,512]{2,1,0:T(8,128)}, u32[]{:S(2)}) copy-start(f32[8,32,512]{2,1,0:T(8,128)} %param.13) | copy-start | bytes 1572868
  240.0 312.7 %copy-start.1 = (f32[8,32,512]{2,1,0:T(8,128)S(1)}, f32[8,32,512]{2,1,0:T(8,128)}, u32[]{:S(2)}) copy-start(f32[8,32,512]{2,1,0:T(8,128)} %param.11) | copy-start | bytes 1572868
  240.0 312.7 %copy-start.2 = (f32[8,32,512]{2,1,0:T(8,128)S(1)}, f32[8,32,512]{2,1,0:T(8,128)}, u32[]{:S(2)}) copy-start(f32[8,32,512]{2,1,0:T(8,128)} %param.12) | copy-start | bytes 1572868
  240.0 422.3 %all-gather.13.cloned.1.call-start = ((), (), s32[]{:S(2)}) async-start(), calls=%async_computation.9 | async-start | bytes 4456448 | tf_op jit(solution)/shard_map/all_gather | solution.py:90
  272.6 344.1 %copy-start.3 = (f32[8,32,512]{2,0,1:T(8,128)S(1)}, f32[8,32,512]{2,0,1:T(8,128)}, u32[]{:S(2)}) copy-start(f32[8,32,512]{2,0,1:T(8,128)} %reduce-scatter.6.cloned.1.call-done) | copy-start | bytes 1572868
  614.4 99.2 %all-gather.17.cloned.1.call-start = ((), (), s32[]{:S(2)}) async-start(), calls=%async_computation.11 | async-start | bytes 4456448 | tf_op jit(solution)/shard_map/all_gather | solution.py:92
  616.4 148.5 %all-gather.15.cloned.1.call-start = ((), (), s32[]{:S(2)}) async-start(), calls=%async_computation.10 | async-start | bytes 4456448 | tf_op jit(solution)/shard_map/all_gather | solution.py:91
Sparse Core Ops, SparseCore 0:
  9.5 53.2 all-gather.10
  65.0 49.0 all-gather.6
  116.3 49.0 all-gather.8
  169.4 103.1 reduce-scatter.5
  276.5 104.4 reduce-scatter.7
  384.9 104.4 reduce-scatter.3
  614.5 47.7 all-gather.12
  664.5 49.0 all-gather.16
  715.8 49.0 all-gather.14
where the time goes:
time: 795 us; the launch traced here: 794 us
  waiting for transfers between devices  472 us (59%)
  matrix products  147 us (18%)
  blocking collectives  118 us (15%)
  local copies, waits for them, and re-layouts  21.1 us (3%)
  other arithmetic  20.9 us (3%)
  between operations  13.3 us (2%)
    reduce_scatter x1, waiting for transfers between devices, on_device(): lax.psum_scatter(grad_gate, ('seq', 'sub'), scatter_dimension=1, tiled=True)  107 us
    reduce_scatter x1, waiting for transfers between devices, on_device(): lax.psum_scatter(grad_down, ('seq', 'sub'), scatter_dimension=1, tiled=True)  107 us
    psum x1, blocking collectives, on_device(): lax.psum((column_squares(fast_gate), column_squares(fast_up), column_squa...  60.4 us
    psum x1, blocking collectives, on_device(): lax.psum((column_squares(moved_all[0]), column_squares(moved_all[1]), col...  57.7 us
    all_gather x1, waiting for transfers between devices, on_device(): lax.all_gather(renewed[1], ('seq', 'sub'), axis=1, tiled=True)  51.2 us
    all_gather x1, waiting for transfers between devices, on_device(): lax.all_gather(fast_gate.astype(jnp.bfloat16), ('seq', 'sub'), axis=1, ti...  47.5 us
    all_gather x1, waiting for transfers between devices, on_device(): lax.all_gather(renewed[0], ('seq', 'sub'), axis=1, tiled=True)  44.6 us
    all_gather x1, waiting for transfers between devices, on_device(): lax.all_gather(fast_down.astype(jnp.bfloat16), ('seq', 'sub'), axis=1, ti...  36.5 us
  transfers between devices with their start and end apart: 9, of which 9 were waited for; matrix products, arithmetic and copies ran while one was open for 20% of the time, Pallas kernels for 0%

commit v1 on v0

--- a/solution.py
+++ b/solution.py
@@ -1,10 +1,371 @@
+import functools
+
 import jax
 import jax.numpy as jnp
 from jax import lax
+from jax.experimental import pallas as pl
+from jax.experimental.pallas import tpu as pltpu
 from jax.sharding import PartitionSpec as P
 
 EPSILON = 1e-06
 STEP_SIZE = 0.5
+WIDTH = 2
+VMEM_LIMIT = 60 * 1024 * 1024
+BF = jnp.bfloat16
+F32 = jnp.float32
+
+
+def place():
+    seq = lax.axis_index("seq")
+    return lax.div(seq, WIDTH), lax.rem(seq, WIDTH), lax.axis_index("sub")
+
+
+def device(z, x, s):
+    return {"seq": z * WIDTH + x, "sub": s}
+
+
+def greet(depth, z, x, s):
+    barrier = pltpu.get_barrier_semaphore()
+    partners = [device(lax.rem(z + k, depth), x, s) for k in range(1, depth)]
+    partners += [device(z, 1 - x, s), device(z, x, 1 - s)]
+    for partner in partners:
+        pl.semaphore_signal(barrier, inc=1, device_id=partner, device_id_type=pl.DeviceIdType.MESH)
+    pl.semaphore_wait(barrier, len(partners))
+
+
+def send(src, dst, send_sem, recv_sem, target):
+    return pltpu.make_async_remote_copy(
+        src_ref=src,
+        dst_ref=dst,
+        send_sem=send_sem,
+        recv_sem=recv_sem,
+        device_id=target,
+        device_id_type=pl.DeviceIdType.MESH,
+    )
+
+
+def gather_kernel(depth, own, full, local, zs, zr, xs, xr, cs, cr):
+    heads = own.shape[0]
+    z, x, s = place()
+    greet(depth, z, x, s)
+    keep = pltpu.make_async_copy(own, full.at[:, :, z, x, s], local)
+    keep.start()
+
+    def along(h, k):
+        return send(
+            own.at[h],
+            full.at[h, :, z, x, s],
+            zs.at[h, k - 1],
+            zr.at[h, k - 1],
+            device(lax.rem(z + k, depth), x, s),
+        )
+
+    def across(h):
+        block = full.at[h, :, :, x, s]
+        return send(block, block, xs.at[h], xr.at[h], device(z, 1 - x, s))
+
+    def inside(h):
+        block = full.at[h, :, :, :, s]
+        return send(block, block, cs.at[h], cr.at[h], device(z, x, 1 - s))
+
+    def first(h, carry):
+        for k in range(1, depth):
+            along(h, k).start()
+        return carry
+
+    lax.fori_loop(0, heads, first, 0)
+    keep.wait()
+
+    def second(h, carry):
+        for k in range(1, depth):
+            along(h, k).wait_recv()
+        across(h).start()
+
+        @pl.when(h > 0)
+        def _():
+            across(h - 1).wait_recv()
+            inside(h - 1).start()
+
+        return carry
+
+    lax.fori_loop(0, heads, second, 0)
+    across(heads - 1).wait_recv()
+    inside(heads - 1).start()
+
+    def last(h, carry):
+        for k in range(1, depth):
+            along(h, k).wait_send()
+        across(h).wait_send()
+        inside(h).wait()
+        return carry
+
+    lax.fori_loop(0, heads, last, 0)
+
+
+def gather(own, depth):
+    heads, kinds, rows, cols = own.shape
+    dma = pltpu.SemaphoreType.DMA
+    full = pl.pallas_call(
+        functools.partial(gather_kernel, depth),
+        out_shape=jax.ShapeDtypeStruct((heads, kinds, depth, WIDTH, 2, rows, cols), own.dtype),
+        in_specs=[pl.BlockSpec(memory_space=pltpu.VMEM)],
+        out_specs=pl.BlockSpec(memory_space=pltpu.VMEM),
+        scratch_shapes=[
+            dma(()),
+            dma((heads, depth - 1)),
+            dma((heads, depth - 1)),
+            dma((heads,)),
+            dma((heads,)),
+            dma((heads,)),
+            dma((heads,)),
+        ],
+        compiler_params=pltpu.CompilerParams(
+            collective_id=0, has_side_effects=True, vmem_limit_bytes=VMEM_LIMIT
+        ),
+        name="gather",
+    )(own)
+    return full.reshape(heads, kinds, depth * WIDTH * 2 * rows, cols)
+
+
+def dot(a, b, dims=((1,), (0,))):
+    return lax.dot_general(a, b, (dims, ((), ())), preferred_element_type=F32)
+
+
+def grads_kernel(keys, values, codes, weights, out):
+    tokens, feats = keys.shape[1:]
+    half = feats // 2
+    rates = (codes[0].astype(F32) + 1.0) / 16.0
+    rates = jnp.transpose(jnp.broadcast_to(rates, (128, tokens)))
+    rates = jnp.concatenate([rates] * (feats // 128), axis=1)
+    target = (-rates * values[0].astype(F32)).astype(BF)
+    k = keys[0]
+    for j in range(2):
+        cols = pl.ds(j * half, half)
+        gate_pre = dot(k, weights[0, 0, :, cols])
+        up_pre = dot(k, weights[0, 1, :, cols])
+        back = dot(target, weights[0, 2, cols, :], ((1,), (1,)))
+        sig = jax.nn.sigmoid(gate_pre)
+        silu = gate_pre * sig
+        hidden = (silu * up_pre).astype(BF)
+        ggp = (back * up_pre * sig * (1.0 + gate_pre * (1.0 - sig))).astype(BF)
+        gup = (back * silu).astype(BF)
+        out[0, j, 0] = dot(k, ggp, ((0,), (0,))).astype(BF)
+        out[0, j, 1] = dot(k, gup, ((0,), (0,))).astype(BF)
+        down = dot(hidden, target, ((0,), (0,))).astype(BF)
+        out[0, 0, 2, cols, :] = down[:, :half]
+        out[0, 1, 2, cols, :] = down[:, half:]
+
+
+def local_grads(keys, values, codes, weights):
+    heads, tokens, feats = keys.shape
+    block = pl.BlockSpec((1, tokens, feats), lambda h: (h, 0, 0))
+    return pl.pallas_call(
+        grads_kernel,
+        grid=(heads,),
+        out_shape=jax.ShapeDtypeStruct((heads, 2, 3, feats, feats // 2), BF),
+        in_specs=[
+            block,
+            block,
+            pl.BlockSpec((1, 1, tokens), lambda h: (h, 0, 0)),
+            pl.BlockSpec((1, 3, feats, feats), lambda h: (h, 0, 0, 0)),
+        ],
+        out_specs=pl.BlockSpec((1, 2, 3, feats, feats // 2), lambda h: (h, 0, 0, 0, 0)),
+        compiler_params=pltpu.CompilerParams(vmem_limit_bytes=VMEM_LIMIT),
+        name="grads",
+    )(keys, values, codes[:, None, :], weights)
+
+
+def apply_kernel(queries, weights, out):
+    q = queries[0]
+    half = weights.shape[-1]
+    total = [None, None]
+    for j in range(2):
+        gate = dot(q, weights[0, j, 0])
+        up = dot(q, weights[0, j, 1])
+        hidden = (gate * jax.nn.sigmoid(gate) * up).astype(BF)
+        for c in range(2):
+            term = dot(hidden, weights[0, c, 2, pl.ds(j * half, half), :])
+            total[c] = term if j == 0 else total[c] + term
+    for c in range(2):
+        out[0, :, pl.ds(c * half, half)] = total[c].astype(BF)
+
+
+def apply_fast(queries, weights):
+    heads, tokens, feats = queries.shape
+    block = pl.BlockSpec((1, tokens, feats), lambda h: (h, 0, 0))
+    return pl.pallas_call(
+        apply_kernel,
+        grid=(heads,),
+        out_shape=jax.ShapeDtypeStruct(queries.shape, BF),
+        in_specs=[
+            block,
+            pl.BlockSpec((1, 2, 3, feats, feats // 2), lambda h: (h, 0, 0, 0, 0)),
+        ],
+        out_specs=block,
+        compiler_params=pltpu.CompilerParams(vmem_limit_bytes=VMEM_LIMIT),
+        name="apply",
+    )(queries, weights)
+
+
+def renew_kernel(
+    depth, grads, weights, new, paired, summed, got_c, got_x, got_z, total, norm_out, norm_in,
+    cs, cr, xs, xr, zs, zr, ns, nr, azs, azr, axs, axr, acs, acr,
+):
+    kinds, rows, half = grads.shape[2:]
+    z, x, s = place()
+    greet(depth, z, x, s)
+
+    def row(k):
+        return lax.rem(z + k, depth)
+
+    def inside(zt, xt):
+        head = zt * WIDTH + xt
+        return send(
+            grads.at[head, 1 - s], got_c.at[head], cs.at[head], cr.at[head], device(z, x, 1 - s)
+        )
+
+    def across(k):
+        return send(paired.at[k], got_x.at[k], xs.at[k], xr.at[k], device(z, 1 - x, s))
+
+    def along(k):
+        return send(
+            summed.at[k - 1], got_z.at[k - 1], zs.at[k - 1], zr.at[k - 1], device(row(k), x, s)
+        )
+
+    order = [k for k in range(1, depth)] + [0]
+    for xt in (1 - x, x):
+        for k in order:
+            inside(row(k), xt).start()
+    for k in order:
+        head = row(k) * WIDTH + 1 - x
+        inside(row(k), 1 - x).wait_recv()
+        for m in range(kinds):
+            paired[k, m] = (grads[head, s, m].astype(F32) + got_c[head, m].astype(F32)).astype(BF)
+        across(k).start()
+    for k in order:
+        head = row(k) * WIDTH + x
+        inside(row(k), x).wait_recv()
+        across(k).wait_recv()
+        if k > 0:
+            for m in range(kinds):
+                both = grads[head, s, m].astype(F32) + got_c[head, m].astype(F32)
+                summed[k - 1, m] = (both + got_x[k, m].astype(F32)).astype(BF)
+            along(k).start()
+    for k in range(1, depth):
+        along(k).wait_recv()
+    mine = z * WIDTH + x
+    for m in range(kinds):
+        part = grads[mine, s, m].astype(F32) + got_c[mine, m].astype(F32)
+        part = part + got_x[0, m].astype(F32)
+        for k in range(1, depth):
+            part = part + got_z[k - 1, m].astype(F32)
+        total[m] = part
+        norm_out[m] = jnp.broadcast_to(jnp.sum(part * part, keepdims=True), norm_out.shape[1:])
+    norms = send(norm_out, norm_in, ns, nr, device(z, x, 1 - s))
+    norms.start()
+    norms.wait()
+
+    def share_z(m, k):
+        block = new.at[z, x, s, m]
+        return send(block, block, azs.at[m, k - 1], azr.at[m, k - 1], device(row(k), x, s))
+
+    def share_x(m, k):
+        block = new.at[lax.rem(z + depth - k, depth), x, s, m]
+        return send(block, block, axs.at[m, k], axr.at[m, k], device(z, 1 - x, s))
+
+    def share_c(m):
+        block = new.at[:, :, s, m]
+        return send(block, block, acs.at[m], acr.at[m], device(z, x, 1 - s))
+
+    for m in range(kinds):
+        whole = weights[m].astype(F32)
+        weight_total = jnp.sum(whole * whole, keepdims=True)
+        grad_total = norm_out[m, :1, :1] + norm_in[m, :1, :1]
+        scale = STEP_SIZE * jnp.sqrt(weight_total + EPSILON) / jnp.sqrt(grad_total + EPSILON)
+        own = weights[m, :, pl.ds(pl.multiple_of(s * half, half), half)].astype(F32)
+        moved = own - scale * total[m]
+        col_weight = jnp.sum(own * own, axis=0, keepdims=True)
+        col_moved = jnp.sum(moved * moved, axis=0, keepdims=True)
+        ratio = jnp.sqrt((col_weight + EPSILON) / (col_moved + EPSILON))
+        new[z, x, s, m] = (moved * ratio).astype(BF)
+        for k in range(1, depth):
+            share_z(m, k).start()
+        share_x(m, 0).start()
+    for m in range(kinds):
+        for k in range(1, depth):
+            share_z(m, k).wait_recv()
+            share_x(m, k).start()
+        if m > 0:
+            for k in range(depth):
+                share_x(m - 1, k).wait_recv()
+            share_c(m - 1).start()
+    for k in range(depth):
+        share_x(kinds - 1, k).wait_recv()
+    share_c(kinds - 1).start()
+
+    for xt in (1 - x, x):
+        for k in order:
+            inside(row(k), xt).wait_send()
+    for k in order:
+        across(k).wait_send()
+    for k in range(1, depth):
+        along(k).wait_send()
+    for m in range(kinds):
+        for k in range(depth):
+            if k > 0:
+                share_z(m, k).wait_send()
+            share_x(m, k).wait_send()
+        share_c(m).wait()
+
+
+def renew(grads, weights, depth):
+    heads, _, kinds, rows, half = grads.shape
+    dma = pltpu.SemaphoreType.DMA
+    piece = (kinds, rows, half)
+    new = pl.pallas_call(
+        functools.partial(renew_kernel, depth),
+        out_shape=jax.ShapeDtypeStruct((depth, WIDTH, 2) + piece, BF),
+        in_specs=[pl.BlockSpec(memory_space=pltpu.VMEM)] * 2,
+        out_specs=pl.BlockSpec(memory_space=pltpu.VMEM),
+        scratch_shapes=[
+            pltpu.VMEM((depth,) + piece, BF),
+            pltpu.VMEM((depth - 1,) + piece, BF),
+            pltpu.VMEM((heads,) + piece, BF),
+            pltpu.VMEM((depth,) + piece, BF),
+            pltpu.VMEM((depth - 1,) + piece, BF),
+            pltpu.VMEM(piece, F32),
+            pltpu.VMEM((kinds, 8, 128), F32),
+            pltpu.VMEM((kinds, 8, 128), F32),
+            dma((heads,)),
+            dma((heads,)),
+            dma((depth,)),
+            dma((depth,)),
+            dma((depth - 1,)),
+            dma((depth - 1,)),
+            dma(()),
+            dma(()),
+            dma((kinds, depth - 1)),
+            dma((kinds, depth - 1)),
+            dma((kinds, depth)),
+            dma((kinds, depth)),
+            dma((kinds,)),
+            dma((kinds,)),
+        ],
+        compiler_params=pltpu.CompilerParams(
+            collective_id=1, has_side_effects=True, vmem_limit_bytes=VMEM_LIMIT
+        ),
+        name="renew",
+    )(grads, weights)
+    return new.reshape((heads, 2) + piece)
+
+
+def on_device_heads(depth, queries, keys, values, lr_codes, fast_gate, fast_up, fast_down):
+    own = jnp.stack([fast_gate, fast_up, fast_down], axis=1).astype(BF)
+    weights = gather(own, depth)
+    grads = local_grads(keys, values, lr_codes, weights)
+    mine = lax.dynamic_index_in_dim(weights, lax.axis_index("seq"), 0, keepdims=False)
+    new = renew(grads, mine, depth)
+    return apply_fast(queries, new)
 
 
 def column_squares(matrix):
@@ -21,7 +382,7 @@
     )
 
 
-def apply_fast(queries, gate_b, up_b, down_b):
+def apply_rows(queries, gate_b, up_b, down_b):
     query_gate = jnp.einsum("htd,hdf->htf", queries, gate_b, preferred_element_type=jnp.float32)
     query_up = jnp.einsum("htd,hdf->htf", queries, up_b, preferred_element_type=jnp.float32)
     query_hidden = (jax.nn.silu(query_gate) * query_up).astype(jnp.bfloat16)
@@ -30,7 +391,7 @@
     ).astype(jnp.bfloat16)
 
 
-def local_grads(keys, target, gate_b, up_b, down_b):
+def local_grads_rows(keys, target, gate_b, up_b, down_b):
     gate_pre = jnp.einsum("htd,hdf->htf", keys, gate_b, preferred_element_type=jnp.float32)
     up_pre = jnp.einsum("htd,hdf->htf", keys, up_b, preferred_element_type=jnp.float32)
     sigmoid_gate = jax.nn.sigmoid(gate_pre)
@@ -46,7 +407,7 @@
     return (grad_gate, grad_up, grad_down)
 
 
-def on_device(queries, keys, values, lr_codes, fast_gate, fast_up, fast_down):
+def on_device_rows(queries, keys, values, lr_codes, fast_gate, fast_up, fast_down):
     token_rates = (lr_codes.astype(jnp.float32) + 1.0) / 16.0
     target = (-token_rates[:, :, None] * values.astype(jnp.float32)).astype(jnp.bfloat16)
     gate_b, up_b, down_b = (
@@ -54,7 +415,7 @@
         lax.all_gather(fast_up.astype(jnp.bfloat16), ("seq", "sub"), axis=1, tiled=True),
         lax.all_gather(fast_down.astype(jnp.bfloat16), ("seq", "sub"), axis=1, tiled=True),
     )
-    grad_gate, grad_up, grad_down = local_grads(keys, target, gate_b, up_b, down_b)
+    grad_gate, grad_up, grad_down = local_grads_rows(keys, target, gate_b, up_b, down_b)
     owned = (
         lax.psum_scatter(grad_gate, ("seq", "sub"), scatter_dimension=1, tiled=True),
         lax.psum_scatter(grad_up, ("seq", "sub"), scatter_dimension=1, tiled=True),
@@ -91,10 +452,17 @@
         lax.all_gather(renewed[1], ("seq", "sub"), axis=1, tiled=True),
         lax.all_gather(renewed[2], ("seq", "sub"), axis=1, tiled=True),
     )
-    return apply_fast(queries, new_gate, new_up, new_down)
+    return apply_rows(queries, new_gate, new_up, new_down)
 
 
 def solution(mesh):
+    seq, sub = mesh.shape["seq"], mesh.shape["sub"]
+
+    def on_device(*arrays):
+        if sub == 2 and seq % WIDTH == 0 and seq > WIDTH and arrays[4].shape[0] == seq:
+            return on_device_heads(seq // WIDTH, *arrays)
+        return on_device_rows(*arrays)
+
     return jax.shard_map(
         on_device,
         mesh=mesh,

time: 795 us -> 366 us (0.46)
  the two profiles are of different devices: /device:TPU:0 before, /device:TPU:17 now
where the time goes in v1:
time: 366 us
  Pallas kernels  358 us (98%)
  local copies, waits for them, and re-layouts  4.05 us (1%)
    pallas_call x1, Pallas kernels, renew(): pl.pallas_call(functools.partial(renew_kernel, depth), out_shape=jax.Shap...  204 us
    pallas_call x1, Pallas kernels, gather(): pl.pallas_call(functools.partial(gather_kernel, depth), out_shape=jax.Sha...  99.7 us
    pallas_call x1, Pallas kernels, local_grads(): pl.pallas_call(grads_kernel, grid=(heads,), out_shape=jax.ShapeDtypeStruc...  36.3 us
    pallas_call x1, Pallas kernels, apply_fast(): pl.pallas_call(apply_kernel, grid=(heads,), out_shape=jax.ShapeDtypeStruc...  18.2 us

profile of v1, /device:TPU:17, one launch (start us, length us, event | category | flops | bytes accessed | tf_op | source)
XLA Modules:
  0.0 365.6 jit_solution(5450512188570248223)
XLA Ops:
  0.0 1.4 broadcast_in_dim.3.codes
  1.4 1.3 convert_bitcast_fusion
  2.7 1.1 convert_bitcast_fusion.2
  3.8 1.0 pad_maximum_fusion.own
  4.7 99.7 %gather.1 = bf16[8,3,4,2,2,32,512]{6,5,4,3,2,1,0:T(8,128)(2,1)} custom-call(bf16[8,3,32,512]{3,2,1,0:T(8,128)(2,1)} %pad_maximum_fusion.own), custom_call_target="tpu_custom_call" | custom-call | tf_op jit(solution)/shard_map/gather/pallas_call | solution.py:108
  104.4 36.3 %grads.1 = bf16[8,2,3,512,256]{4,3,2,1,0:T(8,128)(2,1)} custom-call(bf16[8,1024,512]{2,1,0:T(8,128)(2,1)} %keys.1, bf16[8,1024,512]{2,1,0:T(8,128)(2,1)} %values.1, s32[8,1,1024]{2,1,0:T(1,128)} %broadcast_in_dim.3.codes, bf16[8,3,512,512]{3,2,1,0:T(8,128)(2,1)} %bitcast.10), custom_call_target="tpu_custom_call" | custom-call | tf_op jit(solution)/shard_map/grads/pallas_call | solution.py:162
  140.7 2.7 dynamic-slice_bitcast_fusion.weights
  143.4 204.0 %renew.1 = bf16[4,2,2,3,512,256]{5,4,3,2,1,0:T(8,128)(2,1)} custom-call(bf16[8,2,3,512,256]{4,3,2,1,0:T(8,128)(2,1)} %grads.1, bf16[3,512,512]{2,1,0:T(8,128)(2,1)} %dynamic-slice_bitcast_fusion.weights), custom_call_target="tpu_custom_call" | custom-call | tf_op jit(solution)/shard_map/renew/pallas_call | solution.py:325
  347.4 18.2 %apply.1 = bf16[8,1024,512]{2,1,0:T(8,128)(2,1)} custom-call(bf16[8,1024,512]{2,1,0:T(8,128)(2,1)} %queries.1, bf16[8,2,3,512,256]{4,3,2,1,0:T(8,128)(2,1)} %bitcast.12), custom_call_target="tpu_custom_call" | custom-call | tf_op jit(solution)/shard_map/apply/pallas_call | solution.py:196

commit v2 on v1

--- a/solution.py
+++ b/solution.py
@@ -9,6 +9,7 @@
 
 EPSILON = 1e-06
 STEP_SIZE = 0.5
+KIND = (0, 2, 1)
 WIDTH = 2
 VMEM_LIMIT = 60 * 1024 * 1024
 BF = jnp.bfloat16
@@ -24,10 +25,10 @@
     return {"seq": z * WIDTH + x, "sub": s}
 
 
-def greet(depth, z, x, s):
+def greet(depth, z, x, s, others=()):
     barrier = pltpu.get_barrier_semaphore()
     partners = [device(lax.rem(z + k, depth), x, s) for k in range(1, depth)]
-    partners += [device(z, 1 - x, s), device(z, x, 1 - s)]
+    partners += [device(z, 1 - x, s), device(z, x, 1 - s), *others]
     for partner in partners:
         pl.semaphore_signal(barrier, inc=1, device_id=partner, device_id_type=pl.DeviceIdType.MESH)
     pl.semaphore_wait(barrier, len(partners))
@@ -44,135 +45,215 @@
     )
 
 
-def gather_kernel(depth, own, full, local, zs, zr, xs, xr, cs, cr):
-    heads = own.shape[0]
-    z, x, s = place()
-    greet(depth, z, x, s)
-    keep = pltpu.make_async_copy(own, full.at[:, :, z, x, s], local)
-    keep.start()
-
-    def along(h, k):
-        return send(
-            own.at[h],
-            full.at[h, :, z, x, s],
-            zs.at[h, k - 1],
-            zr.at[h, k - 1],
-            device(lax.rem(z + k, depth), x, s),
-        )
-
-    def across(h):
-        block = full.at[h, :, :, x, s]
-        return send(block, block, xs.at[h], xr.at[h], device(z, 1 - x, s))
-
-    def inside(h):
-        block = full.at[h, :, :, :, s]
-        return send(block, block, cs.at[h], cr.at[h], device(z, x, 1 - s))
-
-    def first(h, carry):
-        for k in range(1, depth):
-            along(h, k).start()
-        return carry
-
-    lax.fori_loop(0, heads, first, 0)
-    keep.wait()
-
-    def second(h, carry):
-        for k in range(1, depth):
-            along(h, k).wait_recv()
-        across(h).start()
-
-        @pl.when(h > 0)
-        def _():
-            across(h - 1).wait_recv()
-            inside(h - 1).start()
-
-        return carry
-
-    lax.fori_loop(0, heads, second, 0)
-    across(heads - 1).wait_recv()
-    inside(heads - 1).start()
-
-    def last(h, carry):
-        for k in range(1, depth):
-            along(h, k).wait_send()
-        across(h).wait_send()
-        inside(h).wait()
-        return carry
-
-    lax.fori_loop(0, heads, last, 0)
-
-
-def gather(own, depth):
-    heads, kinds, rows, cols = own.shape
-    dma = pltpu.SemaphoreType.DMA
-    full = pl.pallas_call(
-        functools.partial(gather_kernel, depth),
-        out_shape=jax.ShapeDtypeStruct((heads, kinds, depth, WIDTH, 2, rows, cols), own.dtype),
-        in_specs=[pl.BlockSpec(memory_space=pltpu.VMEM)],
-        out_specs=pl.BlockSpec(memory_space=pltpu.VMEM),
-        scratch_shapes=[
-            dma(()),
-            dma((heads, depth - 1)),
-            dma((heads, depth - 1)),
-            dma((heads,)),
-            dma((heads,)),
-            dma((heads,)),
-            dma((heads,)),
-        ],
-        compiler_params=pltpu.CompilerParams(
-            collective_id=0, has_side_effects=True, vmem_limit_bytes=VMEM_LIMIT
-        ),
-        name="gather",
-    )(own)
-    return full.reshape(heads, kinds, depth * WIDTH * 2 * rows, cols)
-
-
 def dot(a, b, dims=((1,), (0,))):
     return lax.dot_general(a, b, (dims, ((), ())), preferred_element_type=F32)
 
 
-def grads_kernel(keys, values, codes, weights, out):
-    tokens, feats = keys.shape[1:]
+def chain(depth, z, hop, started, unit, k):
+    for back in (True, False):
+        src = z - k if back else z + k
+        onward = 1 if back else -1
+        here = (src >= 0) if back else (src < depth)
+
+        @pl.when(here)
+        def _(src=src, onward=onward):
+            hop(unit, src, -onward).wait_recv()
+            started(unit, src)
+
+            @pl.when((z + onward >= 0) & (z + onward < depth))
+            def _():
+                hop(unit, src, onward).start()
+
+
+def chain_own(depth, z, hop, unit):
+    for onward in (1, -1):
+
+        @pl.when((z + onward >= 0) & (z + onward < depth))
+        def _(onward=onward):
+            hop(unit, z, onward).start()
+
+
+def chain_sent(depth, z, hop, unit):
+    for src in range(depth):
+
+        @pl.when((src <= z) & (z < depth - 1))
+        def _(src=src):
+            hop(unit, src, 1).wait_send()
+
+        @pl.when((src >= z) & (z > 0))
+        def _(src=src):
+            hop(unit, src, -1).wait_send()
+
+
+def head_grads(k, values, codes, full, h, out):
+    tokens, feats = k.shape
     half = feats // 2
-    rates = (codes[0].astype(F32) + 1.0) / 16.0
+    depth = full.shape[2]
+    rates = (codes.astype(F32) + 1.0) / 16.0
     rates = jnp.transpose(jnp.broadcast_to(rates, (128, tokens)))
     rates = jnp.concatenate([rates] * (feats // 128), axis=1)
-    target = (-rates * values[0].astype(F32)).astype(BF)
-    k = keys[0]
+    target = (-rates * values.astype(F32)).astype(BF)
     for j in range(2):
         cols = pl.ds(j * half, half)
-        gate_pre = dot(k, weights[0, 0, :, cols])
-        up_pre = dot(k, weights[0, 1, :, cols])
-        back = dot(target, weights[0, 2, cols, :], ((1,), (1,)))
+        gate = full[h, 0, :, :, :, :, cols].reshape(feats, half)
+        up = full[h, 2, :, :, :, :, cols].reshape(feats, half)
+        down = full[h, 1, pl.ds(j * (depth // 2), depth // 2)].reshape(half, feats)
+        gate_pre = dot(k, gate)
+        up_pre = dot(k, up)
+        back = dot(target, down, ((1,), (1,)))
         sig = jax.nn.sigmoid(gate_pre)
         silu = gate_pre * sig
         hidden = (silu * up_pre).astype(BF)
         ggp = (back * up_pre * sig * (1.0 + gate_pre * (1.0 - sig))).astype(BF)
         gup = (back * silu).astype(BF)
-        out[0, j, 0] = dot(k, ggp, ((0,), (0,))).astype(BF)
-        out[0, j, 1] = dot(k, gup, ((0,), (0,))).astype(BF)
-        down = dot(hidden, target, ((0,), (0,))).astype(BF)
-        out[0, 0, 2, cols, :] = down[:, :half]
-        out[0, 1, 2, cols, :] = down[:, half:]
-
-
-def local_grads(keys, values, codes, weights):
-    heads, tokens, feats = keys.shape
-    block = pl.BlockSpec((1, tokens, feats), lambda h: (h, 0, 0))
+        out[j, 0] = dot(k, ggp, ((0,), (0,))).astype(BF)
+        out[j, 1] = dot(k, gup, ((0,), (0,))).astype(BF)
+        gdown = dot(hidden, target, ((0,), (0,))).astype(BF)
+        out[0, 2, cols, :] = gdown[:, :half]
+        out[1, 2, cols, :] = gdown[:, half:]
+
+
+def gather_kernel(
+    depth, own, keys, values, codes, grads, mine, full, kbuf, vbuf, obuf,
+    local, ksem, vsem, osem, sr, sl, zr, xs, xr, ys, yr, cs, cr,
+):
+    heads = own.shape[0]
+    z, x, s = place()
+    y = lax.axis_index("groups")
+
+    def load(h):
+        slot = lax.rem(h, 2)
+        return (
+            pltpu.make_async_copy(keys.at[h], kbuf.at[slot], ksem.at[slot]),
+            pltpu.make_async_copy(values.at[h], vbuf.at[slot], vsem.at[slot]),
+        )
+
+    def store(h):
+        slot = lax.rem(h, 2)
+        return pltpu.make_async_copy(obuf.at[slot], grads.at[h], osem.at[slot])
+
+    for copy in load(0) + load(1):
+        copy.start()
+    pair = pl.ds(y, 2)
+    keep = pltpu.make_async_copy(own.at[:, pair], full.at[:, pair, z, x, s], local)
+    keep.start()
+    greet(depth, z, x, s, ({"groups": 1 - y},))
+    keep.wait()
+
+    def hop(h, src, onward):
+        block = full.at[h, pair, src, x, s]
+        sems = sr if onward == 1 else sl
+        return send(block, block, sems.at[h, src], zr.at[h, src], device(z + onward, x, s))
+
+    def across(h, src):
+        block = full.at[h, pair, src, x, s]
+        return send(block, block, xs.at[h, src], xr.at[h, src], device(z, 1 - x, s))
+
+    def over(h):
+        block = full.at[h, 2 * y, :, :, s]
+        return send(block, block, ys.at[h], yr.at[h], {"groups": 1 - y})
+
+    def inside(h):
+        block = full.at[h, :, :, :, s]
+        return send(block, block, cs.at[h], cr.at[h], device(z, x, 1 - s))
+
+    def first(h):
+        chain_own(depth, z, hop, h)
+        across(h, z).start()
+
+    def hand(h):
+        for src in range(depth):
+            across(h, src).wait_recv()
+        over(h).start()
+
+    def spread(h):
+        over(h).wait_recv()
+        inside(h).start()
+
+    def compute(h):
+        slot = lax.rem(h, 2)
+        inside(h).wait_recv()
+        for copy in load(h):
+            copy.wait()
+
+        @pl.when(h >= 2)
+        def _():
+            store(h - 2).wait()
+
+        head_grads(kbuf[slot], vbuf[slot], codes[h], full, h, obuf.at[slot])
+        store(h).start()
+
+        @pl.when(h + 2 < heads)
+        def _():
+            for copy in load(h + 2):
+                copy.start()
+
+    ahead = 2
+    for h in range(ahead):
+        first(h)
+
+    def step(t, carry):
+        def when(h, what):
+            pl.when((h >= 0) & (h < heads))(lambda: what(h))
+
+        when(t + ahead, first)
+        when(t - depth, spread)
+        when(t - depth + 1, hand)
+        for k in range(depth - 1, 0, -1):
+            when(t - k + 1, lambda h, k=k: chain(depth, z, hop, lambda u, i: across(u, i).start(), h, k))
+        when(t - depth - 1, compute)
+        return carry
+
+    lax.fori_loop(0, heads + depth + 1, step, 0)
+    feats = mine.shape[1]
+    for m in range(3):
+        mine[m] = full[z * WIDTH + x, m].reshape(feats, feats)
+
+    def last(h, carry):
+        chain_sent(depth, z, hop, h)
+        for src in range(depth):
+            across(h, src).wait_send()
+        over(h).wait_send()
+        inside(h).wait_send()
+        return carry
+
+    lax.fori_loop(0, heads, last, 0)
+    store(heads - 2).wait()
+    store(heads - 1).wait()
+
+
+def gather_grads(own, keys, values, codes, depth):
+    heads, kinds, rows, cols = own.shape
+    tokens, feats = keys.shape[1:]
+    dma = pltpu.SemaphoreType.DMA
+    vmem = pl.BlockSpec(memory_space=pltpu.VMEM)
+    anywhere = pl.BlockSpec(memory_space=pl.ANY)
+    block = (2, kinds, feats, feats // 2)
     return pl.pallas_call(
-        grads_kernel,
-        grid=(heads,),
-        out_shape=jax.ShapeDtypeStruct((heads, 2, 3, feats, feats // 2), BF),
-        in_specs=[
-            block,
-            block,
-            pl.BlockSpec((1, 1, tokens), lambda h: (h, 0, 0)),
-            pl.BlockSpec((1, 3, feats, feats), lambda h: (h, 0, 0, 0)),
+        functools.partial(gather_kernel, depth),
+        out_shape=(
+            jax.ShapeDtypeStruct((heads,) + block, BF),
+            jax.ShapeDtypeStruct((kinds, feats, feats), BF),
+        ),
+        in_specs=[vmem, anywhere, anywhere, vmem],
+        out_specs=(anywhere, vmem),
+        scratch_shapes=[
+            pltpu.VMEM((heads, kinds, depth, WIDTH, 2, rows, cols), BF),
+            pltpu.VMEM((2, tokens, feats), BF),
+            pltpu.VMEM((2, tokens, feats), BF),
+            pltpu.VMEM((2,) + block, BF),
+            dma(()),
+            dma((2,)),
+            dma((2,)),
+            dma((2,)),
+            *[dma((heads, depth))] * 5,
+            *[dma((heads,))] * 4,
         ],
-        out_specs=pl.BlockSpec((1, 2, 3, feats, feats // 2), lambda h: (h, 0, 0, 0, 0)),
-        compiler_params=pltpu.CompilerParams(vmem_limit_bytes=VMEM_LIMIT),
-        name="grads",
-    )(keys, values, codes[:, None, :], weights)
+        compiler_params=pltpu.CompilerParams(
+            collective_id=0, has_side_effects=True, vmem_limit_bytes=VMEM_LIMIT
+        ),
+        name="gather_grads",
+    )(own, keys, values, codes[:, None, :])
 
 
 def apply_kernel(queries, weights, out):
@@ -209,7 +290,7 @@
 
 def renew_kernel(
     depth, grads, weights, new, paired, summed, got_c, got_x, got_z, total, norm_out, norm_in,
-    cs, cr, xs, xr, zs, zr, ns, nr, azs, azr, axs, axr, acs, acr,
+    cs, cr, xs, xr, zs, zr, ns, nr, asr, asl, azr, axs, axr, acs, acr,
 ):
     kinds, rows, half = grads.shape[2:]
     z, x, s = place()
@@ -265,43 +346,45 @@
     norms.start()
     norms.wait()
 
-    def share_z(m, k):
-        block = new.at[z, x, s, m]
-        return send(block, block, azs.at[m, k - 1], azr.at[m, k - 1], device(row(k), x, s))
-
-    def share_x(m, k):
-        block = new.at[lax.rem(z + depth - k, depth), x, s, m]
-        return send(block, block, axs.at[m, k], axr.at[m, k], device(z, 1 - x, s))
-
-    def share_c(m):
-        block = new.at[:, :, s, m]
-        return send(block, block, acs.at[m], acr.at[m], device(z, x, 1 - s))
+    def hop(m, src, onward):
+        block = new.at[src, x, s, m]
+        sems = asr if onward == 1 else asl
+        return send(block, block, sems.at[m, src], azr.at[m, src], device(z + onward, x, s))
+
+    def share_x(m, src):
+        block = new.at[src, x, s, m]
+        return send(block, block, axs.at[m, src], axr.at[m, src], device(z, 1 - x, s))
+
+    def share_c(m, src):
+        block = new.at[src, :, s, m]
+        return send(block, block, acs.at[m, src], acr.at[m, src], device(z, x, 1 - s))
+
+    def pass_on(m, src):
+        share_x(m, src).wait_recv()
+        share_c(m, src).start()
 
     for m in range(kinds):
-        whole = weights[m].astype(F32)
+        whole = weights[KIND[m]].astype(F32)
         weight_total = jnp.sum(whole * whole, keepdims=True)
         grad_total = norm_out[m, :1, :1] + norm_in[m, :1, :1]
         scale = STEP_SIZE * jnp.sqrt(weight_total + EPSILON) / jnp.sqrt(grad_total + EPSILON)
-        own = weights[m, :, pl.ds(pl.multiple_of(s * half, half), half)].astype(F32)
+        own = weights[KIND[m], :, pl.ds(pl.multiple_of(s * half, half), half)].astype(F32)
         moved = own - scale * total[m]
         col_weight = jnp.sum(own * own, axis=0, keepdims=True)
         col_moved = jnp.sum(moved * moved, axis=0, keepdims=True)
         ratio = jnp.sqrt((col_weight + EPSILON) / (col_moved + EPSILON))
         new[z, x, s, m] = (moved * ratio).astype(BF)
-        for k in range(1, depth):
-            share_z(m, k).start()
-        share_x(m, 0).start()
-    for m in range(kinds):
-        for k in range(1, depth):
-            share_z(m, k).wait_recv()
-            share_x(m, k).start()
-        if m > 0:
-            for k in range(depth):
-                share_x(m - 1, k).wait_recv()
-            share_c(m - 1).start()
-    for k in range(depth):
-        share_x(kinds - 1, k).wait_recv()
-    share_c(kinds - 1).start()
+        chain_own(depth, z, hop, m)
+        share_x(m, z).start()
+    for k in range(1, depth + 1):
+        for m in range(kinds):
+            if k < depth:
+                chain(depth, z, hop, lambda u, i: share_x(u, i).start(), m, k)
+            if k == 1:
+                pass_on(m, z)
+            else:
+                pl.when(z - k + 1 >= 0)(lambda m=m, k=k: pass_on(m, z - k + 1))
+                pl.when(z + k - 1 < depth)(lambda m=m, k=k: pass_on(m, z + k - 1))
 
     for xt in (1 - x, x):
         for k in order:
@@ -311,11 +394,10 @@
     for k in range(1, depth):
         along(k).wait_send()
     for m in range(kinds):
-        for k in range(depth):
-            if k > 0:
-                share_z(m, k).wait_send()
-            share_x(m, k).wait_send()
-        share_c(m).wait()
+        chain_sent(depth, z, hop, m)
+        for src in range(depth):
+            share_x(m, src).wait_send()
+            share_c(m, src).wait()
 
 
 def renew(grads, weights, depth):
@@ -344,12 +426,7 @@
             dma((depth - 1,)),
             dma(()),
             dma(()),
-            dma((kinds, depth - 1)),
-            dma((kinds, depth - 1)),
-            dma((kinds, depth)),
-            dma((kinds, depth)),
-            dma((kinds,)),
-            dma((kinds,)),
+            *[dma((kinds, depth))] * 7,
         ],
         compiler_params=pltpu.CompilerParams(
             collective_id=1, has_side_effects=True, vmem_limit_bytes=VMEM_LIMIT
@@ -360,10 +437,8 @@
 
 
 def on_device_heads(depth, queries, keys, values, lr_codes, fast_gate, fast_up, fast_down):
-    own = jnp.stack([fast_gate, fast_up, fast_down], axis=1).astype(BF)
-    weights = gather(own, depth)
-    grads = local_grads(keys, values, lr_codes, weights)
-    mine = lax.dynamic_index_in_dim(weights, lax.axis_index("seq"), 0, keepdims=False)
+    own = jnp.stack([fast_gate, fast_down, fast_up], axis=1).astype(BF)
+    grads, mine = gather_grads(own, keys, values, lr_codes, depth)
     new = renew(grads, mine, depth)
     return apply_fast(queries, new)
 
@@ -456,10 +531,10 @@
 
 
 def solution(mesh):
-    seq, sub = mesh.shape["seq"], mesh.shape["sub"]
+    groups, seq, sub = (mesh.shape[axis] for axis in ("groups", "seq", "sub"))
 
     def on_device(*arrays):
-        if sub == 2 and seq % WIDTH == 0 and seq > WIDTH and arrays[4].shape[0] == seq:
+        if groups == 2 and sub == 2 and seq % (2 * WIDTH) == 0 and arrays[4].shape[0] == seq:
             return on_device_heads(seq // WIDTH, *arrays)
         return on_device_rows(*arrays)
 

time: 366 us -> 291 us (0.80)
  the two profiles are of different devices: /device:TPU:17 before, /device:TPU:0 now
where the time goes in v2:
time: 291 us; the launch traced here: 289 us
  Pallas kernels  284 us (98%)
  other arithmetic  3.31 us (1%)
    pallas_call x1, Pallas kernels, renew(): pl.pallas_call(functools.partial(renew_kernel, depth), out_shape=jax.Shap...  175 us
    pallas_call x1, Pallas kernels, gather_grads(): pl.pallas_call(functools.partial(gather_kernel, depth), out_shape=(jax.Sh...  91.1 us
    pallas_call x1, Pallas kernels, apply_fast(): pl.pallas_call(apply_kernel, grid=(heads,), out_shape=jax.ShapeDtypeStruc...  18.2 us

profile of v2, /device:TPU:0, one launch (start us, length us, event | category | flops | bytes accessed | tf_op | source)
XLA Modules:
  0.0 288.8 jit_solution(13456326311854010721)
XLA Ops:
  0.0 1.4 broadcast_in_dim.3.codes
  1.4 1.1 convert_bitcast_fusion.2
  2.5 1.3 convert_bitcast_fusion
  3.7 1.0 pad_maximum_fusion.own
  4.7 91.1 %gather_grads.1 = (bf16[8,2,3,512,256]{4,3,2,1,0:T(8,128)(2,1)}, bf16[3,512,512]{2,1,0:T(8,128)(2,1)}) custom-call(bf16[8,3,32,512]{3,2,1,0:T(8,128)(2,1)} %pad_maximum_fusion.own, bf16[8,1024,512]{2,1,0:T(8,128)(2,1)} %keys.1, bf16[8,1024,512]{2,1,0:T(8,128)(2,1)} %values.1, s32[8,1,1024]{2,1,0:T(1,128)} %broadcast_in_dim.3.codes), custom_call_target="tpu_custom_call" | custom-call | tf_op jit(solution)/shard_map/gather_grads/pallas_call | solution.py:232
  95.8 174.8 %renew.1 = bf16[4,2,2,3,512,256]{5,4,3,2,1,0:T(8,128)(2,1)} custom-call(bf16[8,2,3,512,256]{4,3,2,1,0:T(8,128)(2,1)} %get-tuple-element.7.grads, bf16[3,512,512]{2,1,0:T(8,128)(2,1)} %get-tuple-element.8.weights), custom_call_target="tpu_custom_call" | custom-call | tf_op jit(solution)/shard_map/renew/pallas_call | solution.py:407
  270.6 18.2 %apply.1 = bf16[8,1024,512]{2,1,0:T(8,128)(2,1)} custom-call(bf16[8,1024,512]{2,1,0:T(8,128)(2,1)} %queries.1, bf16[8,2,3,512,256]{4,3,2,1,0:T(8,128)(2,1)} %bitcast.7), custom_call_target="tpu_custom_call" | custom-call | tf_op jit(solution)/shard_map/apply/pallas_call | solution.py:277

commit v3 on v2

--- a/solution.py
+++ b/solution.py
@@ -113,9 +113,23 @@
         out[1, 2, cols, :] = gdown[:, half:]
 
 
+def owner(depth, h):
+    pos = h // WIDTH
+    return jnp.where(pos % 2 == 0, pos // 2, depth - 1 - pos // 2)
+
+
+def head_at(depth, h):
+    return owner(depth, h) * WIDTH + h % WIDTH
+
+
+def place_of(depth, z):
+    return jnp.where(2 * z < depth, 2 * z, 2 * (depth - 1 - z) + 1)
+
+
 def gather_kernel(
-    depth, own, keys, values, codes, grads, mine, full, kbuf, vbuf, obuf,
-    local, ksem, vsem, osem, sr, sl, zr, xs, xr, ys, yr, cs, cr,
+    depth, own, keys, values, codes, total, mine,
+    full, kbuf, vbuf, obuf, got_c, paired, kept, got_x, summed, got_z,
+    local, ksem, vsem, sr, sl, zr, xs, xr, ys, yr, cs, cr, gcs, gcr, gxs, gxr, gzs, gzr,
 ):
     heads = own.shape[0]
     z, x, s = place()
@@ -124,13 +138,9 @@
     def load(h):
         slot = lax.rem(h, 2)
         return (
-            pltpu.make_async_copy(keys.at[h], kbuf.at[slot], ksem.at[slot]),
-            pltpu.make_async_copy(values.at[h], vbuf.at[slot], vsem.at[slot]),
+            pltpu.make_async_copy(keys.at[head_at(depth, h)], kbuf.at[slot], ksem.at[slot]),
+            pltpu.make_async_copy(values.at[head_at(depth, h)], vbuf.at[slot], vsem.at[slot]),
         )
-
-    def store(h):
-        slot = lax.rem(h, 2)
-        return pltpu.make_async_copy(obuf.at[slot], grads.at[h], osem.at[slot])
 
     for copy in load(0) + load(1):
         copy.start()
@@ -170,6 +180,53 @@
         over(h).wait_recv()
         inside(h).start()
 
+    def trade(h):
+        return send(
+            obuf.at[lax.rem(h, 2), 1 - s], got_c.at[h], gcs.at[h], gcr.at[h], device(z, x, 1 - s)
+        )
+
+    def deliver(zt):
+        return send(paired.at[zt], got_x.at[zt], gxs.at[zt], gxr.at[zt], device(z, 1 - x, s))
+
+    def along(zt):
+        return send(summed.at[zt], got_z.at[z], gzs.at[zt], gzr.at[z], device(zt, x, s))
+
+    def pair_up(h):
+        zt = owner(depth, h)
+        trade(h).wait_recv()
+        slot = lax.rem(h, 2)
+        ours = lax.rem(h, WIDTH) == x
+
+        @pl.when(ours)
+        def _():
+            for m in range(3):
+                kept[zt, m] = obuf[slot, s, m].astype(F32) + got_c[h, m].astype(F32)
+
+        @pl.when(jnp.logical_not(ours))
+        def _():
+            for m in range(3):
+                both = obuf[slot, s, m].astype(F32) + got_c[h, m].astype(F32)
+                paired[zt, m] = both.astype(BF)
+            deliver(zt).start()
+
+    def join(h):
+        zt = owner(depth, h)
+
+        @pl.when(lax.rem(h, WIDTH) == WIDTH - 1)
+        def _():
+            deliver(zt).wait_recv()
+
+            @pl.when(zt == z)
+            def _():
+                for m in range(3):
+                    total[m] = kept[zt, m] + got_x[zt, m].astype(F32)
+
+            @pl.when(zt != z)
+            def _():
+                for m in range(3):
+                    summed[zt, m] = (kept[zt, m] + got_x[zt, m].astype(F32)).astype(BF)
+                along(zt).start()
+
     def compute(h):
         slot = lax.rem(h, 2)
         inside(h).wait_recv()
@@ -178,10 +235,10 @@
 
         @pl.when(h >= 2)
         def _():
-            store(h - 2).wait()
-
-        head_grads(kbuf[slot], vbuf[slot], codes[h], full, h, obuf.at[slot])
-        store(h).start()
+            trade(h - 2).wait_send()
+
+        head_grads(kbuf[slot], vbuf[slot], codes[head_at(depth, h)], full, h, obuf.at[slot])
+        trade(h).start()
 
         @pl.when(h + 2 < heads)
         def _():
@@ -202,12 +259,22 @@
         for k in range(depth - 1, 0, -1):
             when(t - k + 1, lambda h, k=k: chain(depth, z, hop, lambda u, i: across(u, i).start(), h, k))
         when(t - depth - 1, compute)
+        when(t - depth - 2, pair_up)
+        when(t - depth - 2 - late, join)
         return carry
 
-    lax.fori_loop(0, heads + depth + 1, step, 0)
+    late = 2
+    lax.fori_loop(0, heads + depth + 2 + late, step, 0)
     feats = mine.shape[1]
     for m in range(3):
-        mine[m] = full[z * WIDTH + x, m].reshape(feats, feats)
+        mine[m] = full[place_of(depth, z) * WIDTH + x, m].reshape(feats, feats)
+    for k in range(1, depth):
+        src = lax.rem(z + k, depth)
+        send(
+            summed.at[src], got_z.at[src], gzs.at[src], gzr.at[src], device(src, x, s)
+        ).wait_recv()
+        for m in range(3):
+            total[m] += got_z[src, m].astype(F32)
 
     def last(h, carry):
         chain_sent(depth, z, hop, h)
@@ -218,41 +285,50 @@
         return carry
 
     lax.fori_loop(0, heads, last, 0)
-    store(heads - 2).wait()
-    store(heads - 1).wait()
-
-
-def gather_grads(own, keys, values, codes, depth):
+    trade(heads - 2).wait_send()
+    trade(heads - 1).wait_send()
+    for zt in range(depth):
+        deliver(zt).wait_send()
+        pl.when(zt != z)(lambda zt=zt: along(zt).wait_send())
+
+
+def learn(own, keys, values, codes, depth):
     heads, kinds, rows, cols = own.shape
     tokens, feats = keys.shape[1:]
     dma = pltpu.SemaphoreType.DMA
     vmem = pl.BlockSpec(memory_space=pltpu.VMEM)
     anywhere = pl.BlockSpec(memory_space=pl.ANY)
-    block = (2, kinds, feats, feats // 2)
+    piece = (kinds, feats, feats // 2)
     return pl.pallas_call(
         functools.partial(gather_kernel, depth),
         out_shape=(
-            jax.ShapeDtypeStruct((heads,) + block, BF),
+            jax.ShapeDtypeStruct(piece, F32),
             jax.ShapeDtypeStruct((kinds, feats, feats), BF),
         ),
         in_specs=[vmem, anywhere, anywhere, vmem],
-        out_specs=(anywhere, vmem),
+        out_specs=(vmem, vmem),
         scratch_shapes=[
             pltpu.VMEM((heads, kinds, depth, WIDTH, 2, rows, cols), BF),
             pltpu.VMEM((2, tokens, feats), BF),
             pltpu.VMEM((2, tokens, feats), BF),
-            pltpu.VMEM((2,) + block, BF),
+            pltpu.VMEM((2, 2) + piece, BF),
+            pltpu.VMEM((heads,) + piece, BF),
+            pltpu.VMEM((depth,) + piece, BF),
+            pltpu.VMEM((depth,) + piece, F32),
+            pltpu.VMEM((depth,) + piece, BF),
+            pltpu.VMEM((depth,) + piece, BF),
+            pltpu.VMEM((depth,) + piece, BF),
             dma(()),
             dma((2,)),
             dma((2,)),
-            dma((2,)),
             *[dma((heads, depth))] * 5,
-            *[dma((heads,))] * 4,
+            *[dma((heads,))] * 6,
+            *[dma((depth,))] * 4,
         ],
         compiler_params=pltpu.CompilerParams(
             collective_id=0, has_side_effects=True, vmem_limit_bytes=VMEM_LIMIT
         ),
-        name="gather_grads",
+        name="learn",
     )(own, keys, values, codes[:, None, :])
 
 
@@ -289,58 +365,13 @@
 
 
 def renew_kernel(
-    depth, grads, weights, new, paired, summed, got_c, got_x, got_z, total, norm_out, norm_in,
-    cs, cr, xs, xr, zs, zr, ns, nr, asr, asl, azr, axs, axr, acs, acr,
+    depth, total, weights, new, norm_out, norm_in, ns, nr, asr, asl, azr, axs, axr, acs, acr
 ):
-    kinds, rows, half = grads.shape[2:]
+    kinds, _, half = total.shape
     z, x, s = place()
     greet(depth, z, x, s)
-
-    def row(k):
-        return lax.rem(z + k, depth)
-
-    def inside(zt, xt):
-        head = zt * WIDTH + xt
-        return send(
-            grads.at[head, 1 - s], got_c.at[head], cs.at[head], cr.at[head], device(z, x, 1 - s)
-        )
-
-    def across(k):
-        return send(paired.at[k], got_x.at[k], xs.at[k], xr.at[k], device(z, 1 - x, s))
-
-    def along(k):
-        return send(
-            summed.at[k - 1], got_z.at[k - 1], zs.at[k - 1], zr.at[k - 1], device(row(k), x, s)
-        )
-
-    order = [k for k in range(1, depth)] + [0]
-    for xt in (1 - x, x):
-        for k in order:
-            inside(row(k), xt).start()
-    for k in order:
-        head = row(k) * WIDTH + 1 - x
-        inside(row(k), 1 - x).wait_recv()
-        for m in range(kinds):
-            paired[k, m] = (grads[head, s, m].astype(F32) + got_c[head, m].astype(F32)).astype(BF)
-        across(k).start()
-    for k in order:
-        head = row(k) * WIDTH + x
-        inside(row(k), x).wait_recv()
-        across(k).wait_recv()
-        if k > 0:
-            for m in range(kinds):
-                both = grads[head, s, m].astype(F32) + got_c[head, m].astype(F32)
-                summed[k - 1, m] = (both + got_x[k, m].astype(F32)).astype(BF)
-            along(k).start()
-    for k in range(1, depth):
-        along(k).wait_recv()
-    mine = z * WIDTH + x
     for m in range(kinds):
-        part = grads[mine, s, m].astype(F32) + got_c[mine, m].astype(F32)
-        part = part + got_x[0, m].astype(F32)
-        for k in range(1, depth):
-            part = part + got_z[k - 1, m].astype(F32)
-        total[m] = part
+        part = total[m]
         norm_out[m] = jnp.broadcast_to(jnp.sum(part * part, keepdims=True), norm_out.shape[1:])
     norms = send(norm_out, norm_in, ns, nr, device(z, x, 1 - s))
     norms.start()
@@ -386,13 +417,6 @@
                 pl.when(z - k + 1 >= 0)(lambda m=m, k=k: pass_on(m, z - k + 1))
                 pl.when(z + k - 1 < depth)(lambda m=m, k=k: pass_on(m, z + k - 1))
 
-    for xt in (1 - x, x):
-        for k in order:
-            inside(row(k), xt).wait_send()
-    for k in order:
-        across(k).wait_send()
-    for k in range(1, depth):
-        along(k).wait_send()
     for m in range(kinds):
         chain_sent(depth, z, hop, m)
         for src in range(depth):
@@ -400,8 +424,8 @@
             share_c(m, src).wait()
 
 
-def renew(grads, weights, depth):
-    heads, _, kinds, rows, half = grads.shape
+def renew(total, weights, depth):
+    kinds, rows, half = total.shape
     dma = pltpu.SemaphoreType.DMA
     piece = (kinds, rows, half)
     new = pl.pallas_call(
@@ -410,20 +434,8 @@
         in_specs=[pl.BlockSpec(memory_space=pltpu.VMEM)] * 2,
         out_specs=pl.BlockSpec(memory_space=pltpu.VMEM),
         scratch_shapes=[
-            pltpu.VMEM((depth,) + piece, BF),
-            pltpu.VMEM((depth - 1,) + piece, BF),
-            pltpu.VMEM((heads,) + piece, BF),
-            pltpu.VMEM((depth,) + piece, BF),
-            pltpu.VMEM((depth - 1,) + piece, BF),
-            pltpu.VMEM(piece, F32),
             pltpu.VMEM((kinds, 8, 128), F32),
             pltpu.VMEM((kinds, 8, 128), F32),
-            dma((heads,)),
-            dma((heads,)),
-            dma((depth,)),
-            dma((depth,)),
-            dma((depth - 1,)),
-            dma((depth - 1,)),
             dma(()),
             dma(()),
             *[dma((kinds, depth))] * 7,
@@ -432,14 +444,17 @@
             collective_id=1, has_side_effects=True, vmem_limit_bytes=VMEM_LIMIT
         ),
         name="renew",
-    )(grads, weights)
-    return new.reshape((heads, 2) + piece)
+    )(total, weights)
+    return new.reshape((depth * WIDTH, 2) + piece)
 
 
 def on_device_heads(depth, queries, keys, values, lr_codes, fast_gate, fast_up, fast_down):
     own = jnp.stack([fast_gate, fast_down, fast_up], axis=1).astype(BF)
-    grads, mine = gather_grads(own, keys, values, lr_codes, depth)
-    new = renew(grads, mine, depth)
+    rows = [p // 2 if p % 2 == 0 else depth - 1 - p // 2 for p in range(depth)]
+    order = [r * WIDTH + x for r in rows for x in range(WIDTH)]
+    own = jnp.stack([own[h] for h in order])
+    total, mine = learn(own, keys, values, lr_codes, depth)
+    new = renew(total, mine, depth)
     return apply_fast(queries, new)
 
 

time: 291 us -> 263 us (0.904)
  Pallas kernels: 284 us -> 257 us
    pallas_call x1, Pallas kernels: 175 us -> 83.3 us  [renew(): pl.pallas_call(functools.partial(renew_kernel, depth), out_shape=jax.Shap...]
    pallas_call x1, Pallas kernels: 91.1 us -> 155 us  [learn(): pl.pallas_call(functools.partial(gather_kernel, depth), out_shape=(jax.Sh...]
where the time goes in v3:
time: 263 us; the launch traced here: 262 us
  Pallas kernels  257 us (98%)
  other arithmetic  3.28 us (1%)
    pallas_call x1, Pallas kernels, learn(): pl.pallas_call(functools.partial(gather_kernel, depth), out_shape=(jax.Sh...  155 us
    pallas_call x1, Pallas kernels, renew(): pl.pallas_call(functools.partial(renew_kernel, depth), out_shape=jax.Shap...  83.3 us
    pallas_call x1, Pallas kernels, apply_fast(): pl.pallas_call(apply_kernel, grid=(heads,), out_shape=jax.ShapeDtypeStruc...  18.2 us

profile of v3, /device:TPU:0, one launch (start us, length us, event | category | flops | bytes accessed | tf_op | source)
XLA Modules:
  0.0 261.7 jit_solution(16875690799841372500)
XLA Ops:
  0.0 1.4 broadcast_in_dim.3.codes
  1.4 1.1 convert_bitcast_fusion.2
  2.5 1.3 convert_bitcast_fusion
  3.7 0.9 fusion.13.own
  4.7 155.5 %learn.1 = (f32[3,512,256]{2,1,0:T(8,128)}, bf16[3,512,512]{2,1,0:T(8,128)(2,1)}) custom-call(bf16[8,3,32,512]{3,2,1,0:T(8,128)(2,1)} %fusion.13.own, bf16[8,1024,512]{2,1,0:T(8,128)(2,1)} %keys.1, bf16[8,1024,512]{2,1,0:T(8,128)(2,1)} %values.1, s32[8,1,1024]{2,1,0:T(1,128)} %broadcast_in_dim.3.codes), custom_call_target="tpu_custom_call" | custom-call | tf_op jit(solution)/shard_map/learn/pallas_call | solution.py:302
  160.2 83.3 %renew.1 = bf16[4,2,2,3,512,256]{5,4,3,2,1,0:T(8,128)(2,1)} custom-call(f32[3,512,256]{2,1,0:T(8,128)} %get-tuple-element.7.total, bf16[3,512,512]{2,1,0:T(8,128)(2,1)} %get-tuple-element.8.weights), custom_call_target="tpu_custom_call" | custom-call | tf_op jit(solution)/shard_map/renew/pallas_call | solution.py:431
  243.5 18.2 %apply.1 = bf16[8,1024,512]{2,1,0:T(8,128)(2,1)} custom-call(bf16[8,1024,512]{2,1,0:T(8,128)(2,1)} %queries.1, bf16[8,2,3,512,256]{4,3,2,1,0:T(8,128)(2,1)} %bitcast.7), custom_call_target="tpu_custom_call" | custom-call | tf_op jit(solution)/shard_map/apply/pallas_call | solution.py:353

commit v4 on v3

--- a/solution.py
+++ b/solution.py
@@ -185,11 +185,15 @@
             obuf.at[lax.rem(h, 2), 1 - s], got_c.at[h], gcs.at[h], gcr.at[h], device(z, x, 1 - s)
         )
 
-    def deliver(zt):
-        return send(paired.at[zt], got_x.at[zt], gxs.at[zt], gxr.at[zt], device(z, 1 - x, s))
-
-    def along(zt):
-        return send(summed.at[zt], got_z.at[z], gzs.at[zt], gzr.at[z], device(zt, x, s))
+    def deliver(zt, m):
+        return send(
+            paired.at[zt, m], got_x.at[zt, m], gxs.at[zt, m], gxr.at[zt, m], device(z, 1 - x, s)
+        )
+
+    def along(zt, m):
+        return send(
+            summed.at[zt, m], got_z.at[z, m], gzs.at[zt, m], gzr.at[z, m], device(zt, x, s)
+        )
 
     def pair_up(h):
         zt = owner(depth, h)
@@ -207,25 +211,25 @@
             for m in range(3):
                 both = obuf[slot, s, m].astype(F32) + got_c[h, m].astype(F32)
                 paired[zt, m] = both.astype(BF)
-            deliver(zt).start()
+                deliver(zt, m).start()
 
     def join(h):
         zt = owner(depth, h)
 
         @pl.when(lax.rem(h, WIDTH) == WIDTH - 1)
         def _():
-            deliver(zt).wait_recv()
-
             @pl.when(zt == z)
             def _():
                 for m in range(3):
+                    deliver(zt, m).wait_recv()
                     total[m] = kept[zt, m] + got_x[zt, m].astype(F32)
 
             @pl.when(zt != z)
             def _():
                 for m in range(3):
+                    deliver(zt, m).wait_recv()
                     summed[zt, m] = (kept[zt, m] + got_x[zt, m].astype(F32)).astype(BF)
-                along(zt).start()
+                    along(zt, m).start()
 
     def compute(h):
         slot = lax.rem(h, 2)
@@ -270,10 +274,11 @@
         mine[m] = full[place_of(depth, z) * WIDTH + x, m].reshape(feats, feats)
     for k in range(1, depth):
         src = lax.rem(z + k, depth)
-        send(
-            summed.at[src], got_z.at[src], gzs.at[src], gzr.at[src], device(src, x, s)
-        ).wait_recv()
         for m in range(3):
+            send(
+                summed.at[src, m], got_z.at[src, m], gzs.at[src, m], gzr.at[src, m],
+                device(src, x, s),
+            ).wait_recv()
             total[m] += got_z[src, m].astype(F32)
 
     def last(h, carry):
@@ -288,8 +293,9 @@
     trade(heads - 2).wait_send()
     trade(heads - 1).wait_send()
     for zt in range(depth):
-        deliver(zt).wait_send()
-        pl.when(zt != z)(lambda zt=zt: along(zt).wait_send())
+        for m in range(3):
+            deliver(zt, m).wait_send()
+            pl.when(zt != z)(lambda zt=zt, m=m: along(zt, m).wait_send())
 
 
 def learn(own, keys, values, codes, depth):
@@ -323,7 +329,7 @@
             dma((2,)),
             *[dma((heads, depth))] * 5,
             *[dma((heads,))] * 6,
-            *[dma((depth,))] * 4,
+            *[dma((depth, kinds))] * 4,
         ],
         compiler_params=pltpu.CompilerParams(
             collective_id=0, has_side_effects=True, vmem_limit_bytes=VMEM_LIMIT
@@ -367,7 +373,7 @@
 def renew_kernel(
     depth, total, weights, new, norm_out, norm_in, ns, nr, asr, asl, azr, axs, axr, acs, acr
 ):
-    kinds, _, half = total.shape
+    kinds, rows, half = total.shape
     z, x, s = place()
     greet(depth, z, x, s)
     for m in range(kinds):
@@ -377,24 +383,37 @@
     norms.start()
     norms.wait()
 
-    def hop(m, src, onward):
-        block = new.at[src, x, s, m]
+    part = rows // 2
+    units = ((2, part, rows - part, True), (2, 0, part, False), (0, 0, rows, False), (1, 0, rows, False))
+
+    def block(u, src, col):
+        m, begin, count, _ = units[u]
+        return new.at[src, col, s, m, pl.ds(begin, count)]
+
+    def hop(unit, src, onward):
+        u, c = unit
+        piece = block(u, src, 1 - x if c else x)
         sems = asr if onward == 1 else asl
-        return send(block, block, sems.at[m, src], azr.at[m, src], device(z + onward, x, s))
-
-    def share_x(m, src):
-        block = new.at[src, x, s, m]
-        return send(block, block, axs.at[m, src], axr.at[m, src], device(z, 1 - x, s))
-
-    def share_c(m, src):
-        block = new.at[src, :, s, m]
-        return send(block, block, acs.at[m, src], acr.at[m, src], device(z, x, 1 - s))
-
-    def pass_on(m, src):
-        share_x(m, src).wait_recv()
-        share_c(m, src).start()
-
-    for m in range(kinds):
+        return send(piece, piece, sems.at[u, c, src], azr.at[u, c, src], device(z + onward, x, s))
+
+    def share_x(u, src):
+        piece = block(u, src, x)
+        return send(piece, piece, axs.at[u, src], axr.at[u, src], device(z, 1 - x, s))
+
+    def share_c(u, src):
+        piece = block(u, src, slice(None))
+        return send(piece, piece, acs.at[u, src], acr.at[u, src], device(z, x, 1 - s))
+
+    def pass_on(u, src):
+        if not units[u][3]:
+            share_x(u, src).wait_recv()
+        share_c(u, src).start()
+
+    def arrived(unit, src):
+        if not units[unit[0]][3]:
+            share_x(unit[0], src).start()
+
+    for m in (2, 0, 1):
         whole = weights[KIND[m]].astype(F32)
         weight_total = jnp.sum(whole * whole, keepdims=True)
         grad_total = norm_out[m, :1, :1] + norm_in[m, :1, :1]
@@ -405,23 +424,32 @@
         col_moved = jnp.sum(moved * moved, axis=0, keepdims=True)
         ratio = jnp.sqrt((col_weight + EPSILON) / (col_moved + EPSILON))
         new[z, x, s, m] = (moved * ratio).astype(BF)
-        chain_own(depth, z, hop, m)
-        share_x(m, z).start()
+        for u in range(len(units)):
+            if units[u][0] == m:
+                share_x(u, z).start()
+                chain_own(depth, z, hop, (u, 0))
+    share_x(0, z).wait_recv()
+    chain_own(depth, z, hop, (0, 1))
     for k in range(1, depth + 1):
-        for m in range(kinds):
+        for u in (1, 2, 3, 0):
             if k < depth:
-                chain(depth, z, hop, lambda u, i: share_x(u, i).start(), m, k)
+                for c in range(2 if units[u][3] else 1):
+                    chain(depth, z, hop, arrived, (u, c), k)
             if k == 1:
-                pass_on(m, z)
+                pass_on(u, z)
             else:
-                pl.when(z - k + 1 >= 0)(lambda m=m, k=k: pass_on(m, z - k + 1))
-                pl.when(z + k - 1 < depth)(lambda m=m, k=k: pass_on(m, z + k - 1))
-
-    for m in range(kinds):
-        chain_sent(depth, z, hop, m)
+                pl.when(z - k + 1 >= 0)(lambda u=u, k=k: pass_on(u, z - k + 1))
+                pl.when(z + k - 1 < depth)(lambda u=u, k=k: pass_on(u, z + k - 1))
+
+    for u in range(len(units)):
+        for c in range(2 if units[u][3] else 1):
+            chain_sent(depth, z, hop, (u, c))
+        if units[u][3]:
+            share_x(u, z).wait_send()
         for src in range(depth):
-            share_x(m, src).wait_send()
-            share_c(m, src).wait()
+            if not units[u][3]:
+                share_x(u, src).wait_send()
+            share_c(u, src).wait()
 
 
 def renew(total, weights, depth):
@@ -438,7 +466,8 @@
             pltpu.VMEM((kinds, 8, 128), F32),
             dma(()),
             dma(()),
-            *[dma((kinds, depth))] * 7,
+            *[dma((4, 2, depth))] * 3,
+            *[dma((4, depth))] * 4,
         ],
         compiler_params=pltpu.CompilerParams(
             collective_id=1, has_side_effects=True, vmem_limit_bytes=VMEM_LIMIT

time: 263 us -> 257 us (0.977)
  Pallas kernels: 257 us -> 251 us
    pallas_call x1, Pallas kernels: 83.3 us -> 77.6 us  [renew(): pl.pallas_call(functools.partial(renew_kernel, depth), out_shape=jax.Shap...]
where the time goes in v4:
time: 257 us; the launch traced here: 256 us
  Pallas kernels  251 us (98%)
  other arithmetic  3.28 us (1%)
    pallas_call x1, Pallas kernels, learn(): pl.pallas_call(functools.partial(gather_kernel, depth), out_shape=(jax.Sh...  156 us
    pallas_call x1, Pallas kernels, renew(): pl.pallas_call(functools.partial(renew_kernel, depth), out_shape=jax.Shap...  77.6 us
    pallas_call x1, Pallas kernels, apply_fast(): pl.pallas_call(apply_kernel, grid=(heads,), out_shape=jax.ShapeDtypeStruc...  18.2 us

profile of v4, /device:TPU:0, one launch (start us, length us, event | category | flops | bytes accessed | tf_op | source)
XLA Modules:
  0.0 256.1 jit_solution(11082226915661433239)
XLA Ops:
  0.0 1.4 broadcast_in_dim.3.codes
  1.4 1.1 convert_bitcast_fusion.2
  2.5 1.3 convert_bitcast_fusion
  3.7 0.9 fusion.13.own
  4.7 155.6 %learn.1 = (f32[3,512,256]{2,1,0:T(8,128)}, bf16[3,512,512]{2,1,0:T(8,128)(2,1)}) custom-call(bf16[8,3,32,512]{3,2,1,0:T(8,128)(2,1)} %fusion.13.own, bf16[8,1024,512]{2,1,0:T(8,128)(2,1)} %keys.1, bf16[8,1024,512]{2,1,0:T(8,128)(2,1)} %values.1, s32[8,1,1024]{2,1,0:T(1,128)} %broadcast_in_dim.3.codes), custom_call_target="tpu_custom_call" | custom-call | tf_op jit(solution)/shard_map/learn/pallas_call | solution.py:308
  160.3 77.6 %renew.1 = bf16[4,2,2,3,512,256]{5,4,3,2,1,0:T(8,128)(2,1)} custom-call(f32[3,512,256]{2,1,0:T(8,128)} %get-tuple-element.7.total, bf16[3,512,512]{2,1,0:T(8,128)(2,1)} %get-tuple-element.8.weights), custom_call_target="tpu_custom_call" | custom-call | tf_op jit(solution)/shard_map/renew/pallas_call | solution.py:459
  237.9 18.2 %apply.1 = bf16[8,1024,512]{2,1,0:T(8,128)(2,1)} custom-call(bf16[8,1024,512]{2,1,0:T(8,128)(2,1)} %queries.1, bf16[8,2,3,512,256]{4,3,2,1,0:T(8,128)(2,1)} %bitcast.7), custom_call_target="tpu_custom_call" | custom-call | tf_op jit(solution)/shard_map/apply/pallas_call | solution.py:359

commit v5 on v4

--- a/solution.py
+++ b/solution.py
@@ -262,8 +262,8 @@
         when(t - depth + 1, hand)
         for k in range(depth - 1, 0, -1):
             when(t - k + 1, lambda h, k=k: chain(depth, z, hop, lambda u, i: across(u, i).start(), h, k))
+        when(t - depth - 2, pair_up)
         when(t - depth - 1, compute)
-        when(t - depth - 2, pair_up)
         when(t - depth - 2 - late, join)
         return carry
 

time: 257 us -> 259 us (level)
  Pallas kernels: 251 us -> 254 us
where the time goes in v5:
time: 259 us
  Pallas kernels  254 us (98%)
  other arithmetic  3.28 us (1%)
    pallas_call x1, Pallas kernels, learn(): pl.pallas_call(functools.partial(gather_kernel, depth), out_shape=(jax.Sh...  158 us
    pallas_call x1, Pallas kernels, renew(): pl.pallas_call(functools.partial(renew_kernel, depth), out_shape=jax.Shap...  77.9 us
    pallas_call x1, Pallas kernels, apply_fast(): pl.pallas_call(apply_kernel, grid=(heads,), out_shape=jax.ShapeDtypeStruc...  18.2 us

profile of v5, /device:TPU:0, one launch (start us, length us, event | category | flops | bytes accessed | tf_op | source)
XLA Modules:
  0.0 258.6 jit_solution(15665687079757466579)
XLA Ops:
  0.0 1.4 broadcast_in_dim.3.codes
  1.4 1.1 convert_bitcast_fusion.2
  2.5 1.3 convert_bitcast_fusion
  3.7 0.9 fusion.13.own
  4.7 157.8 %learn.1 = (f32[3,512,256]{2,1,0:T(8,128)}, bf16[3,512,512]{2,1,0:T(8,128)(2,1)}) custom-call(bf16[8,3,32,512]{3,2,1,0:T(8,128)(2,1)} %fusion.13.own, bf16[8,1024,512]{2,1,0:T(8,128)(2,1)} %keys.1, bf16[8,1024,512]{2,1,0:T(8,128)(2,1)} %values.1, s32[8,1,1024]{2,1,0:T(1,128)} %broadcast_in_dim.3.codes), custom_call_target="tpu_custom_call" | custom-call | tf_op jit(solution)/shard_map/learn/pallas_call | solution.py:308
  162.5 77.9 %renew.1 = bf16[4,2,2,3,512,256]{5,4,3,2,1,0:T(8,128)(2,1)} custom-call(f32[3,512,256]{2,1,0:T(8,128)} %get-tuple-element.7.total, bf16[3,512,512]{2,1,0:T(8,128)(2,1)} %get-tuple-element.8.weights), custom_call_target="tpu_custom_call" | custom-call | tf_op jit(solution)/shard_map/renew/pallas_call | solution.py:459
  240.4 18.2 %apply.1 = bf16[8,1024,512]{2,1,0:T(8,128)(2,1)} custom-call(bf16[8,1024,512]{2,1,0:T(8,128)(2,1)} %queries.1, bf16[8,2,3,512,256]{4,3,2,1,0:T(8,128)(2,1)} %bitcast.7), custom_call_target="tpu_custom_call" | custom-call | tf_op jit(solution)/shard_map/apply/pallas_call | solution.py:359
